TPU v7x, 256 devices: a whole 4x4x8 slice. The times are simulated.
256 devices in a mesh: row: 32 (over x_hi, z, core), col: 8 (over y, x_lo).
Axes of the slice: x: 4 (x_hi: 2, x_lo: 2; x = x_hi * 2 + x_lo), y: 4, z: 8, core: 2. Of those that a mesh axis runs over, the one named last changes fastest.
Arguments:
- features: bfloat16 [65536, 256], P(('row', 'col')), may hold values from -6 to 6
- degrees: int32 [65536], P(('row', 'col')), may hold values from 1 to 64
- blocks: bfloat16 [1024, 88, 128, 128], P('row', 'col'), may hold values from 0 to 2
- block_ids: int32 [1024, 88], P('row', 'col'), may hold values from 0 to 31, as said below
- counts: int32 [1024, 8], P('row', 'col'), may hold values from 1 to 11, as said below
- weight: bfloat16 [256, 256], replicated, may hold values from -0.375 to 0.375
- out_bias: float32 [256], replicated, may hold values from -3 to 3
Outputs:
- mixed: bfloat16 [65536, 256], P(('row', 'col'))
Inputs may be any that keep to these rules, and one draw needn't show every extreme that they name: `block_ids`: within each list of 11 slots (live or not) the codes are distinct. `counts`: every tile has one segment whose list is full.
All inputs are finite; a program needn't handle non-finite values.
Results may differ from a plain program's by a relative error of at most 0.018.
Values may be sent and summed in bfloat16 or wider, within the bound.
A program may use at most 128 MiB of HBM per device.

v0:
```python
import jax
import jax.numpy as jnp
from jax import lax
from jax.sharding import PartitionSpec as P


def slot_term(block_vals, slot_codes, low_slot, high_slot, gathered, seg_rows):
    block_side = block_vals.shape[1]
    col_blocks = gathered.shape[0] // block_side
    row_blocks = seg_rows // block_side
    feat_width = gathered.shape[1]
    col_place = slot_codes % col_blocks
    row_place = slot_codes // col_blocks
    pieces = jnp.take(gathered.reshape(col_blocks, block_side, feat_width), col_place, axis=0)
    products = jnp.einsum("kij,kjf->kif", block_vals, pieces, preferred_element_type=jnp.float32)
    slot_place = jnp.arange(slot_codes.shape[0], dtype=jnp.int32)
    occupied = (slot_place >= low_slot) & (slot_place < high_slot)
    select = (
        (row_place[:, None] == jnp.arange(row_blocks, dtype=jnp.int32)[None, :]) & occupied[:, None]
    ).astype(jnp.float32)
    summed = jnp.einsum("kr,kif->rif", select, products, precision=lax.Precision.HIGHEST)
    return summed.reshape(seg_rows, feat_width)


def local(features, degrees, blocks, block_ids, counts, weight, out_bias):
    scaling = lax.rsqrt(degrees.astype(jnp.float32))[:, None]
    scaled = (features.astype(jnp.float32) * scaling).astype(jnp.bfloat16)
    gathered = lax.all_gather(scaled, "col", axis=0, tiled=True)
    seg_rows = features.shape[0]
    sub_count = lax.axis_size("row")

    def segment_term(subrange):
        block_vals = lax.dynamic_index_in_dim(blocks, subrange, 0, keepdims=False)
        slot_codes = lax.dynamic_index_in_dim(block_ids, subrange, 0, keepdims=False)
        live_count = lax.dynamic_index_in_dim(counts, subrange, 0, keepdims=False)[0]
        return slot_term(block_vals, slot_codes, 0, live_count, gathered, seg_rows)

    partial_value = lax.map(segment_term, jnp.arange(sub_count, dtype=jnp.int32), batch_size=4)
    summed = lax.psum_scatter(
        partial_value.reshape(sub_count * seg_rows, partial_value.shape[2]).astype(jnp.bfloat16),
        "row",
        scatter_dimension=0,
        tiled=True,
    ).astype(jnp.float32)
    combined = (scaling * (summed + scaled.astype(jnp.float32))).astype(jnp.bfloat16)
    mixed = jnp.dot(combined, weight, preferred_element_type=jnp.float32) + out_bias
    return jnp.maximum(mixed, 0.0).astype(jnp.bfloat16)


def solution(mesh):
    placed = (
        P(("row", "col"), None),
        P(("row", "col")),
        P("row", "col", None, None),
        P("row", "col"),
        P("row", "col"),
        P(),
        P(),
    )
    return jax.shard_map(
        local, mesh=mesh, in_specs=placed, out_specs=P(("row", "col"), None), check_vma=False
    )
```

profile of v0, /device:TPU:1, one launch (start us, length us, event | category | flops | bytes accessed | tf_op | source)
XLA Modules:
  0.0 381.0 jit_solution(8092162391961774073)
XLA Ops:
  9.8 41.7 %all-gather.2.cloned.1.call-done = bf16[2048,256]{1,0:T(8,128)(2,1)} async-done(((bf16[256,256]{1,0:T(8,128)(2,1)}), bf16[2048,256]{1,0:T(8,128)(2,1)}) %all-gather.2.cloned.1.call-update) | async-done | bytes 1048592 | tf_op jit(solution)/shard_map/all_gather | solution.py:28
  51.5 193.7 %while.12 = (s32[]{:T(128)}, bf16[8,4,256,256]{3,2,1,0:T(8,128)(2,1)}, s32[8,4]{1,0:T(8,128)S(1)}, s32[32,11]{1,0:T(8,128)S(1)}, s32[32,1]{0,1:T(1,128)}, /*inde...) while((s32[]{:T(128)}, bf16[8,4,256,256]{3,2,1,0:T(8,128)(2,1)}, ...), condition=%wide.region_1.2_spmd, body=%wide.region_0.1_spmd.sunk | while | flops 405146816 | bytes 27139636 | solution.py:38
  52.2 2.0 gather_fusion.2
  54.2 6.1 %gather_fusion = bf16[4,11,128,128]{3,2,1,0:T(8,128)(2,1)} fusion(bf16[32,11,128,128]{3,2,1,0:T(8,128)(2,1)} %get-tuple-element.190, s32[4]{0:T(128)S(1)} %fusion.34), kind=kCustom, calls=%fused_computation.2.clone.1 | custom fusion | bytes 2883648 | tf_op jit(solution)/shard_map/while/body/eval_jaxpr/vmap(jit(dynamic_index_in_dim))/gather | solution.py:33
  60.3 4.8 %fusion.35 = f32[4,11,128,256]{3,2,1,0:T(8,128)} fusion(bf16[4,11,128,128]{3,2,1,0:T(8,128)(2,1)} %gather_fusion, bf16[4,11,128,256]{3,2,1,0:T(8,128)(2,1)S(1)} %bitcast.37, pred[4,11]{1,0:T(4,128)(4,1)S(1)} %compare_and_fusion.2), kind=kOutput, calls=%fused_computation.6.clone.1 | convolution fusion | flops 370540544 | bytes 10092588 | tf_op jit(solution)/shard_map/while/body/eval_jaxpr/vmap(kij,kjf->kif)/dot_general | solution.py:15
  65.9 8.9 %fusion.36 = bf16[4,2,128,256]{3,1,2,0:T(2,128)(2,1)S(1)} fusion(f32[4,11,128,256]{3,2,1,0:T(8,128)} %fusion.35, pred[4,11]{1,0:T(4,128)(4,1)S(1)} %iota_compare_fusion.2, s32[4,11]{1,0:T(4,128)S(1)} %add_select_fusion.4), kind=kOutput, calls=%fused_computation.4.clone.1 | convolution fusion | flops 34603184 | bytes 6291676 | tf_op jit(solution)/shard_map/while/body/eval_jaxpr/vmap(kr,kif->rif)/dot_general | solution.py:21
  76.4 2.0 gather_fusion.2
  78.4 6.1 %gather_fusion = bf16[4,11,128,128]{3,2,1,0:T(8,128)(2,1)} fusion(bf16[32,11,128,128]{3,2,1,0:T(8,128)(2,1)} %get-tuple-element.190, s32[4]{0:T(128)S(1)} %fusion.34), kind=kCustom, calls=%fused_computation.2.clone.1 | custom fusion | bytes 2883648 | tf_op jit(solution)/shard_map/while/body/eval_jaxpr/vmap(jit(dynamic_index_in_dim))/gather | solution.py:33
  84.5 4.8 %fusion.35 = f32[4,11,128,256]{3,2,1,0:T(8,128)} fusion(bf16[4,11,128,128]{3,2,1,0:T(8,128)(2,1)} %gather_fusion, bf16[4,11,128,256]{3,2,1,0:T(8,128)(2,1)S(1)} %bitcast.37, pred[4,11]{1,0:T(4,128)(4,1)S(1)} %compare_and_fusion.2), kind=kOutput, calls=%fused_computation.6.clone.1 | convolution fusion | flops 370540544 | bytes 10092588 | tf_op jit(solution)/shard_map/while/body/eval_jaxpr/vmap(kij,kjf->kif)/dot_general | solution.py:15
  90.0 8.9 %fusion.36 = bf16[4,2,128,256]{3,1,2,0:T(2,128)(2,1)S(1)} fusion(f32[4,11,128,256]{3,2,1,0:T(8,128)} %fusion.35, pred[4,11]{1,0:T(4,128)(4,1)S(1)} %iota_compare_fusion.2, s32[4,11]{1,0:T(4,128)S(1)} %add_select_fusion.4), kind=kOutput, calls=%fused_computation.4.clone.1 | convolution fusion | flops 34603184 | bytes 6291676 | tf_op jit(solution)/shard_map/while/body/eval_jaxpr/vmap(kr,kif->rif)/dot_general | solution.py:21
  100.6 2.0 gather_fusion.2
  102.6 6.1 %gather_fusion = bf16[4,11,128,128]{3,2,1,0:T(8,128)(2,1)} fusion(bf16[32,11,128,128]{3,2,1,0:T(8,128)(2,1)} %get-tuple-element.190, s32[4]{0:T(128)S(1)} %fusion.34), kind=kCustom, calls=%fused_computation.2.clone.1 | custom fusion | bytes 2883648 | tf_op jit(solution)/shard_map/while/body/eval_jaxpr/vmap(jit(dynamic_index_in_dim))/gather | solution.py:33
  108.7 4.8 %fusion.35 = f32[4,11,128,256]{3,2,1,0:T(8,128)} fusion(bf16[4,11,128,128]{3,2,1,0:T(8,128)(2,1)} %gather_fusion, bf16[4,11,128,256]{3,2,1,0:T(8,128)(2,1)S(1)} %bitcast.37, pred[4,11]{1,0:T(4,128)(4,1)S(1)} %compare_and_fusion.2), kind=kOutput, calls=%fused_computation.6.clone.1 | convolution fusion | flops 370540544 | bytes 10092588 | tf_op jit(solution)/shard_map/while/body/eval_jaxpr/vmap(kij,kjf->kif)/dot_general | solution.py:15
  114.3 8.9 %fusion.36 = bf16[4,2,128,256]{3,1,2,0:T(2,128)(2,1)S(1)} fusion(f32[4,11,128,256]{3,2,1,0:T(8,128)} %fusion.35, pred[4,11]{1,0:T(4,128)(4,1)S(1)} %iota_compare_fusion.2, s32[4,11]{1,0:T(4,128)S(1)} %add_select_fusion.4), kind=kOutput, calls=%fused_computation.4.clone.1 | convolution fusion | flops 34603184 | bytes 6291676 | tf_op jit(solution)/shard_map/while/body/eval_jaxpr/vmap(kr,kif->rif)/dot_general | solution.py:21
  124.8 2.0 gather_fusion.2
  126.8 6.1 %gather_fusion = bf16[4,11,128,128]{3,2,1,0:T(8,128)(2,1)} fusion(bf16[32,11,128,128]{3,2,1,0:T(8,128)(2,1)} %get-tuple-element.190, s32[4]{0:T(128)S(1)} %fusion.34), kind=kCustom, calls=%fused_computation.2.clone.1 | custom fusion | bytes 2883648 | tf_op jit(solution)/shard_map/while/body/eval_jaxpr/vmap(jit(dynamic_index_in_dim))/gather | solution.py:33
  132.9 4.8 %fusion.35 = f32[4,11,128,256]{3,2,1,0:T(8,128)} fusion(bf16[4,11,128,128]{3,2,1,0:T(8,128)(2,1)} %gather_fusion, bf16[4,11,128,256]{3,2,1,0:T(8,128)(2,1)S(1)} %bitcast.37, pred[4,11]{1,0:T(4,128)(4,1)S(1)} %compare_and_fusion.2), kind=kOutput, calls=%fused_computation.6.clone.1 | convolution fusion | flops 370540544 | bytes 10092588 | tf_op jit(solution)/shard_map/while/body/eval_jaxpr/vmap(kij,kjf->kif)/dot_general | solution.py:15
  138.5 8.9 %fusion.36 = bf16[4,2,128,256]{3,1,2,0:T(2,128)(2,1)S(1)} fusion(f32[4,11,128,256]{3,2,1,0:T(8,128)} %fusion.35, pred[4,11]{1,0:T(4,128)(4,1)S(1)} %iota_compare_fusion.2, s32[4,11]{1,0:T(4,128)S(1)} %add_select_fusion.4), kind=kOutput, calls=%fused_computation.4.clone.1 | convolution fusion | flops 34603184 | bytes 6291676 | tf_op jit(solution)/shard_map/while/body/eval_jaxpr/vmap(kr,kif->rif)/dot_general | solution.py:21
  151.0 6.1 %gather_fusion = bf16[4,11,128,128]{3,2,1,0:T(8,128)(2,1)} fusion(bf16[32,11,128,128]{3,2,1,0:T(8,128)(2,1)} %get-tuple-element.190, s32[4]{0:T(128)S(1)} %fusion.34), kind=kCustom, calls=%fused_computation.2.clone.1 | custom fusion | bytes 2883648 | tf_op jit(solution)/shard_map/while/body/eval_jaxpr/vmap(jit(dynamic_index_in_dim))/gather | solution.py:33
  157.1 4.8 %fusion.35 = f32[4,11,128,256]{3,2,1,0:T(8,128)} fusion(bf16[4,11,128,128]{3,2,1,0:T(8,128)(2,1)} %gather_fusion, bf16[4,11,128,256]{3,2,1,0:T(8,128)(2,1)S(1)} %bitcast.37, pred[4,11]{1,0:T(4,128)(4,1)S(1)} %compare_and_fusion.2), kind=kOutput, calls=%fused_computation.6.clone.1 | convolution fusion | flops 370540544 | bytes 10092588 | tf_op jit(solution)/shard_map/while/body/eval_jaxpr/vmap(kij,kjf->kif)/dot_general | solution.py:15
  162.7 8.9 %fusion.36 = bf16[4,2,128,256]{3,1,2,0:T(2,128)(2,1)S(1)} fusion(f32[4,11,128,256]{3,2,1,0:T(8,128)} %fusion.35, pred[4,11]{1,0:T(4,128)(4,1)S(1)} %iota_compare_fusion.2, s32[4,11]{1,0:T(4,128)S(1)} %add_select_fusion.4), kind=kOutput, calls=%fused_computation.4.clone.1 | convolution fusion | flops 34603184 | bytes 6291676 | tf_op jit(solution)/shard_map/while/body/eval_jaxpr/vmap(kr,kif->rif)/dot_general | solution.py:21
  173.2 2.0 gather_fusion.2
  175.2 6.1 %gather_fusion = bf16[4,11,128,128]{3,2,1,0:T(8,128)(2,1)} fusion(bf16[32,11,128,128]{3,2,1,0:T(8,128)(2,1)} %get-tuple-element.190, s32[4]{0:T(128)S(1)} %fusion.34), kind=kCustom, calls=%fused_computation.2.clone.1 | custom fusion | bytes 2883648 | tf_op jit(solution)/shard_map/while/body/eval_jaxpr/vmap(jit(dynamic_index_in_dim))/gather | solution.py:33
  181.3 4.8 %fusion.35 = f32[4,11,128,256]{3,2,1,0:T(8,128)} fusion(bf16[4,11,128,128]{3,2,1,0:T(8,128)(2,1)} %gather_fusion, bf16[4,11,128,256]{3,2,1,0:T(8,128)(2,1)S(1)} %bitcast.37, pred[4,11]{1,0:T(4,128)(4,1)S(1)} %compare_and_fusion.2), kind=kOutput, calls=%fused_computation.6.clone.1 | convolution fusion | flops 370540544 | bytes 10092588 | tf_op jit(solution)/shard_map/while/body/eval_jaxpr/vmap(kij,kjf->kif)/dot_general | solution.py:15
  186.9 8.9 %fusion.36 = bf16[4,2,128,256]{3,1,2,0:T(2,128)(2,1)S(1)} fusion(f32[4,11,128,256]{3,2,1,0:T(8,128)} %fusion.35, pred[4,11]{1,0:T(4,128)(4,1)S(1)} %iota_compare_fusion.2, s32[4,11]{1,0:T(4,128)S(1)} %add_select_fusion.4), kind=kOutput, calls=%fused_computation.4.clone.1 | convolution fusion | flops 34603184 | bytes 6291676 | tf_op jit(solution)/shard_map/while/body/eval_jaxpr/vmap(kr,kif->rif)/dot_general | solution.py:21
  199.5 6.1 %gather_fusion = bf16[4,11,128,128]{3,2,1,0:T(8,128)(2,1)} fusion(bf16[32,11,128,128]{3,2,1,0:T(8,128)(2,1)} %get-tuple-element.190, s32[4]{0:T(128)S(1)} %fusion.34), kind=kCustom, calls=%fused_computation.2.clone.1 | custom fusion | bytes 2883648 | tf_op jit(solution)/shard_map/while/body/eval_jaxpr/vmap(jit(dynamic_index_in_dim))/gather | solution.py:33
  205.6 4.8 %fusion.35 = f32[4,11,128,256]{3,2,1,0:T(8,128)} fusion(bf16[4,11,128,128]{3,2,1,0:T(8,128)(2,1)} %gather_fusion, bf16[4,11,128,256]{3,2,1,0:T(8,128)(2,1)S(1)} %bitcast.37, pred[4,11]{1,0:T(4,128)(4,1)S(1)} %compare_and_fusion.2), kind=kOutput, calls=%fused_computation.6.clone.1 | convolution fusion | flops 370540544 | bytes 10092588 | tf_op jit(solution)/shard_map/while/body/eval_jaxpr/vmap(kij,kjf->kif)/dot_general | solution.py:15
  211.1 8.9 %fusion.36 = bf16[4,2,128,256]{3,1,2,0:T(2,128)(2,1)S(1)} fusion(f32[4,11,128,256]{3,2,1,0:T(8,128)} %fusion.35, pred[4,11]{1,0:T(4,128)(4,1)S(1)} %iota_compare_fusion.2, s32[4,11]{1,0:T(4,128)S(1)} %add_select_fusion.4), kind=kOutput, calls=%fused_computation.4.clone.1 | convolution fusion | flops 34603184 | bytes 6291676 | tf_op jit(solution)/shard_map/while/body/eval_jaxpr/vmap(kr,kif->rif)/dot_general | solution.py:21
  223.7 6.1 %gather_fusion = bf16[4,11,128,128]{3,2,1,0:T(8,128)(2,1)} fusion(bf16[32,11,128,128]{3,2,1,0:T(8,128)(2,1)} %get-tuple-element.190, s32[4]{0:T(128)S(1)} %fusion.34), kind=kCustom, calls=%fused_computation.2.clone.1 | custom fusion | bytes 2883648 | tf_op jit(solution)/shard_map/while/body/eval_jaxpr/vmap(jit(dynamic_index_in_dim))/gather | solution.py:33
  229.8 4.8 %fusion.35 = f32[4,11,128,256]{3,2,1,0:T(8,128)} fusion(bf16[4,11,128,128]{3,2,1,0:T(8,128)(2,1)} %gather_fusion, bf16[4,11,128,256]{3,2,1,0:T(8,128)(2,1)S(1)} %bitcast.37, pred[4,11]{1,0:T(4,128)(4,1)S(1)} %compare_and_fusion.2), kind=kOutput, calls=%fused_computation.6.clone.1 | convolution fusion | flops 370540544 | bytes 10092588 | tf_op jit(solution)/shard_map/while/body/eval_jaxpr/vmap(kij,kjf->kif)/dot_general | solution.py:15
  235.4 8.9 %fusion.36 = bf16[4,2,128,256]{3,1,2,0:T(2,128)(2,1)S(1)} fusion(f32[4,11,128,256]{3,2,1,0:T(8,128)} %fusion.35, pred[4,11]{1,0:T(4,128)(4,1)S(1)} %iota_compare_fusion.2, s32[4,11]{1,0:T(4,128)S(1)} %add_select_fusion.4), kind=kOutput, calls=%fused_computation.4.clone.1 | convolution fusion | flops 34603184 | bytes 6291676 | tf_op jit(solution)/shard_map/while/body/eval_jaxpr/vmap(kr,kif->rif)/dot_general | solution.py:21
  245.3 127.1 %reduce-scatter.2.cloned.1.call-done = bf16[256,256]{1,0:T(8,128)(2,1)} async-done(((bf16[8192,256]{1,0:T(8,128)(2,1)}), bf16[256,256]{1,0:T(8,128)(2,1)}) %reduce-scatter.2.cloned.1.call-update) | async-done | bytes 131088 | tf_op jit(solution)/shard_map/reduce_scatter | solution.py:39
  (123 shorter events, 29.7 us)
Async XLA Ops:
  6.5 365.8 %copy-start = (bf16[256,256]{1,0:T(8,128)(2,1)S(1)}, bf16[256,256]{1,0:T(8,128)(2,1)}, u32[]{:S(2)}) copy-start(bf16[256,256]{1,0:T(8,128)(2,1)} %param.14) | copy-start | bytes 393220
  6.5 45.0 %all-gather.2.cloned.1.call-start = ((), (), s32[]{:S(2)}) async-start(), calls=%async_computation.1 | async-start | bytes 1179648 | tf_op jit(solution)/shard_map/all_gather | solution.py:28
  8.9 363.4 %reduce-scatter.2.cloned.1.call-start = ((), (), s32[]{:S(2)}) async-start(), calls=%async_computation.2 | async-start | bytes 4325376 | tf_op jit(solution)/shard_map/reduce_scatter | solution.py:39
  60.3 4.8 %copy-start.1 = (s32[32,1]{0,1:T(1,128)S(1)}, s32[32,1]{0,1:T(1,128)}, u32[]{:S(2)}) copy-start(s32[32,1]{0,1:T(1,128)} %get-tuple-element.189) | copy-start | bytes 388 | tf_op jit(solution)/shard_map/while
  84.5 4.8 %copy-start.1 = (s32[32,1]{0,1:T(1,128)S(1)}, s32[32,1]{0,1:T(1,128)}, u32[]{:S(2)}) copy-start(s32[32,1]{0,1:T(1,128)} %get-tuple-element.189) | copy-start | bytes 388 | tf_op jit(solution)/shard_map/while
  108.7 4.8 %copy-start.1 = (s32[32,1]{0,1:T(1,128)S(1)}, s32[32,1]{0,1:T(1,128)}, u32[]{:S(2)}) copy-start(s32[32,1]{0,1:T(1,128)} %get-tuple-element.189) | copy-start | bytes 388 | tf_op jit(solution)/shard_map/while
  132.9 4.8 %copy-start.1 = (s32[32,1]{0,1:T(1,128)S(1)}, s32[32,1]{0,1:T(1,128)}, u32[]{:S(2)}) copy-start(s32[32,1]{0,1:T(1,128)} %get-tuple-element.189) | copy-start | bytes 388 | tf_op jit(solution)/shard_map/while
  157.1 4.8 %copy-start.1 = (s32[32,1]{0,1:T(1,128)S(1)}, s32[32,1]{0,1:T(1,128)}, u32[]{:S(2)}) copy-start(s32[32,1]{0,1:T(1,128)} %get-tuple-element.189) | copy-start | bytes 388 | tf_op jit(solution)/shard_map/while
  181.3 4.8 %copy-start.1 = (s32[32,1]{0,1:T(1,128)S(1)}, s32[32,1]{0,1:T(1,128)}, u32[]{:S(2)}) copy-start(s32[32,1]{0,1:T(1,128)} %get-tuple-element.189) | copy-start | bytes 388 | tf_op jit(solution)/shard_map/while
  205.6 4.8 %copy-start.1 = (s32[32,1]{0,1:T(1,128)S(1)}, s32[32,1]{0,1:T(1,128)}, u32[]{:S(2)}) copy-start(s32[32,1]{0,1:T(1,128)} %get-tuple-element.189) | copy-start | bytes 388 | tf_op jit(solution)/shard_map/while
  229.8 4.8 %copy-start.1 = (s32[32,1]{0,1:T(1,128)S(1)}, s32[32,1]{0,1:T(1,128)}, u32[]{:S(2)}) copy-start(s32[32,1]{0,1:T(1,128)} %get-tuple-element.189) | copy-start | bytes 388 | tf_op jit(solution)/shard_map/while
  245.2 127.1 %copy-start.2 = (bf16[256,256]{1,0:T(8,128)(2,1)S(1)}, bf16[256,256]{1,0:T(8,128)(2,1)}, u32[]{:S(2)}) copy-start(bf16[256,256]{1,0:T(8,128)(2,1)} %param.9) | copy-start | bytes 393220
  245.2 127.1 %copy-start.3 = (f32[256]{0:T(256)S(1)}, f32[256]{0:T(256)}, u32[]{:S(2)}) copy-start(f32[256]{0:T(256)} %param.15) | copy-start | bytes 3076
Sparse Core Ops, SparseCore 0:
  9.1 42.2 all-gather.1
  245.4 126.9 reduce-scatter.1
where the time goes:
time: 386 us; the launch traced here: 381 us
  waiting for transfers between devices  169 us (44%)
  matrix products  112 us (29%)
  local copies, waits for them, and re-layouts  83.2 us (22%)
  between operations  13.4 us (3%)
    reduce_scatter x1, waiting for transfers between devices, local(): lax.psum_scatter(partial_value.reshape(sub_count * seg_rows, partial_valu...  127 us
    dot_general x8, matrix products, slot_term(): jnp.einsum('kr,kif->rif', select, products, precision=lax.Precision.HIGHEST)  71.3 us
    gather x8, local copies, waits for them, and re-layouts, segment_term(): block_vals = lax.dynamic_index_in_dim(blocks, subrange, 0, keepdims=False)  49 us
    all_gather x1, waiting for transfers between devices, local(): gathered = lax.all_gather(scaled, 'col', axis=0, tiled=True)  41.7 us
    dot_general x8, matrix products, slot_term(): jnp.einsum('kij,kjf->kif', block_vals, pieces, preferred_element_type=jnp...  38.6 us
    gather x8, local copies, waits for them, and re-layouts, slot_term(): jnp.take(gathered.reshape(col_blocks, block_side, feat_width), col_place,...  15.7 us
  transfers between devices with their start and end apart: 2, of which 2 were waited for; matrix products, arithmetic and copies ran while one was open for 0% of the time, Pallas kernels for 0%

commit v1 on v0

v1 whole, which is shorter than its diff:
```python
import functools

import jax
import jax.numpy as jnp
from jax import lax
from jax.experimental import pallas as pl
from jax.experimental.pallas import tpu as pltpu
from jax.sharding import PartitionSpec as P

MESH = pl.DeviceIdType.MESH
BF = jnp.bfloat16
F32 = jnp.float32
NZ = 8
NY = 4
SEGS = 32
SLOTS = 11
BS = 128
ROWS = 256
FEAT = 256
WAVE = [0, 0, 0, 1, 0, 0, 1, 1, 0, 0, 1, 1, 0, 1, 1, 1]
DIST = [4, 3, -3, 4, 2, -2, 3, -3, 1, -1, 2, -2, 0, 1, -1, 0]
TASK = {(w, d): i for i, (w, d) in enumerate(zip(WAVE, DIST))}


def pick(table, index):
    value = jnp.int32(table[0])
    for i in range(1, len(table)):
        value = jnp.where(index >= i, jnp.int32(table[i]), value)
    return value


def kernel(
    deg_ref, feat_ref, blocks_ref, ids_ref, cnt_ref, weight_ref, bias_ref, out_ref,
    gat, stage, left, own, sib_out, sib_in, z_out, z_in, z_in2, x_out, x_in, scal,
    stage_sem, ag_send, ag_recv, sib_send, sib_recv, z_send, z_recv, z_send2, z_recv2, x_send, x_recv,
):
    row, col = lax.axis_index("row"), lax.axis_index("col")
    core = row % 2
    z = (row // 2) % NZ
    xh = row // (2 * NZ)
    y, xl = col // 2, col % 2

    def at(xh_, z_, core_):
        return xh_ * (2 * NZ) + z_ * 2 + core_

    z_up = (at(xh, (z + 1) % NZ, core), col)
    z_dn = (at(xh, (z + NZ - 1) % NZ, core), col)
    sib = (at(xh, z, 1 - core), col)
    x_far = (at(1 - xh, z, core), col)
    c_up = ((y + 1) % NY) * 2 + xl
    c_dn = ((y + NY - 1) % NY) * 2 + xl
    c_x = y * 2 + 1 - xl
    c_two = ((y + 2) % NY) * 2 + xl
    y_up, y_dn, x_near = (row, c_up), (row, c_dn), (row, c_x)
    cx_up = ((y + 1) % NY) * 2 + 1 - xl
    cx_dn = ((y + NY - 1) % NY) * 2 + 1 - xl
    cx_two = ((y + 2) % NY) * 2 + 1 - xl

    barrier = pltpu.get_barrier_semaphore()
    for other in (z_up, z_dn, sib, x_far, y_up, y_dn, x_near):
        pl.semaphore_signal(barrier, inc=1, device_id=other, device_id_type=MESH)

    loads = [
        pltpu.make_async_copy(
            blocks_ref.at[pl.ds(4 * i, 4)], stage.at[pl.ds(4 * i, 4)], stage_sem.at[i]
        )
        for i in range(8)
    ]
    for load in loads:
        load.start()

    rows = lax.broadcasted_iota(jnp.int32, (ROWS, ROWS), 0)
    cols = lax.broadcasted_iota(jnp.int32, (ROWS, ROWS), 1)
    degs = jnp.broadcast_to(deg_ref[...].astype(F32), (ROWS, ROWS))
    scaling = lax.rsqrt(jnp.sum(jnp.where(rows == cols, degs, 0.0), axis=1, keepdims=True))
    scal[...] = scaling
    scaled = (feat_ref[...].astype(F32) * scaling).astype(BF)
    gat[2 * col] = scaled[:BS]
    gat[2 * col + 1] = scaled[BS:]

    pl.semaphore_wait(barrier, 7)

    def ag(source, half, send, recv, target):
        block = gat.at[2 * source + half]
        return pltpu.make_async_remote_copy(
            src_ref=block, dst_ref=block, send_sem=ag_send.at[send], recv_sem=ag_recv.at[recv],
            device_id=target, device_id_type=MESH,
        )

    def landed(source, half, recv):
        ag(source, half, 0, recv, y_up).wait_recv()

    sends = []
    for half in (0, 1):
        sends += [
            ag(col, half, half, half, y_up),
            ag(col, half, 2 + half, 2 + half, y_dn),
            ag(col, half, 4 + half, 4 + half, x_near),
        ]
    for copy in sends:
        copy.start()

    def prepare(first, last):
        for i in range(first // 4, last // 4):
            loads[i].wait()

        def body(s, carry):
            live = cnt_ref[s, 0]
            for k in range(SLOTS):
                q = ids_ref[s, k]
                block = stage[s, k]
                top = jnp.where((q < 16) & (k < live), 1.0, 0.0).astype(F32)
                low = jnp.where((q >= 16) & (k < live), 1.0, 0.0).astype(F32)
                left[s, :BS, k * BS:(k + 1) * BS] = block * jnp.full((BS, BS), top, F32).astype(BF)
                left[s, BS:, k * BS:(k + 1) * BS] = block * jnp.full((BS, BS), low, F32).astype(BF)
            return carry

        lax.fori_loop(first, last, body, 0)

    prepare(0, 12)

    def relay(source, half, recv, *copies):
        landed(source, half, recv)
        for copy in copies:
            copy.start()
            sends.append(copy)

    relay(c_dn, 0, 0, ag(c_dn, 0, 6, 6, y_up))
    relay(c_x, 0, 4, ag(c_x, 0, 8, 8, y_up), ag(c_x, 0, 10, 10, y_dn))
    relay(c_up, 1, 3, ag(c_up, 1, 7, 7, y_dn))
    relay(c_x, 1, 5, ag(c_x, 1, 9, 9, y_up), ag(c_x, 1, 11, 11, y_dn))
    prepare(12, 24)
    relay(c_two, 0, 6, ag(c_two, 0, 12, 12, x_near))
    relay(c_two, 1, 7, ag(c_two, 1, 13, 13, x_near))
    prepare(24, 32)
    landed(c_dn, 1, 1)
    landed(c_up, 0, 2)
    for half in (0, 1):
        landed(cx_dn, half, 8 + half)
        landed(cx_up, half, 10 + half)
        landed(cx_two, half, 12 + half)

    def term(s):
        right = jnp.concatenate([gat[ids_ref[s, k] % 16] for k in range(SLOTS)], axis=0)
        return jnp.dot(left[s], right, preferred_element_type=F32)

    def sib_copy(i):
        return pltpu.make_async_remote_copy(
            src_ref=sib_out.at[i], dst_ref=sib_in.at[i], send_sem=sib_send.at[i], recv_sem=sib_recv.at[i],
            device_id=sib, device_id_type=MESH,
        )

    def z_copy(task, half=None):
        w, d = WAVE[task], DIST[task]
        if d == 4:
            then, target = (TASK[w, 3], z_up) if half == 0 else (TASK[w, -3], z_dn)
            part = pl.ds(half * BS, BS)
            second = half == 1
            return pltpu.make_async_remote_copy(
                src_ref=z_out.at[task, part], dst_ref=z_in.at[then, part],
                send_sem=(z_send2 if second else z_send).at[w if second else task], recv_sem=z_recv.at[then],
                device_id=target, device_id_type=MESH,
            )
        then, target = (TASK[w, d - 1], z_up) if d > 0 else (TASK[w, d + 1], z_dn)
        if d == -1:
            dst, recv = z_in2.at[w], z_recv2.at[w]
        else:
            dst, recv = z_in.at[then], z_recv.at[then]
        return pltpu.make_async_remote_copy(
            src_ref=z_out.at[task], dst_ref=dst, send_sem=z_send.at[task], recv_sem=recv,
            device_id=target, device_id_type=MESH,
        )

    x_copy = pltpu.make_async_remote_copy(
        src_ref=x_out, dst_ref=x_in, send_sem=x_send, recv_sem=x_recv, device_id=x_far, device_id_type=MESH
    )

    def finish(i):
        w, d = WAVE[i], DIST[i]
        sib_copy(i).wait_recv()
        if d == 3:
            z_copy(TASK[w, 4], 0).wait_recv()
        elif d == -3:
            z_copy(TASK[w, 4], 1).wait_recv()
        elif d > 0 and d < 3:
            z_copy(TASK[w, d + 1]).wait_recv()
        elif d < 0:
            z_copy(TASK[w, d - 1]).wait_recv()
        elif d == 0:
            z_copy(TASK[w, 1]).wait_recv()
            z_copy(TASK[w, -1]).wait_recv()
        if i == 15:
            return
        dest = x_out if d == 0 else z_out.at[i]
        for half in (0, 1):
            part = pl.ds(half * BS, BS)
            value = own[i, part] + sib_in[i, part].astype(F32)
            if d in (1, 2, -1, -2, 0) or (d == 3 and half == 0) or (d == -3 and half == 1):
                value = value + z_in[i, part].astype(F32)
            if d == 0:
                value = value + z_in2[w, part].astype(F32)
            dest[part] = value.astype(BF)
        if d == 4:
            z_copy(i, 0).start()
            z_copy(i, 1).start()
        elif d == 0:
            x_copy.start()
        else:
            z_copy(i).start()

    def step(i, carry):
        @pl.when(i < 16)
        def _():
            w, d = pick(WAVE, i), pick(DIST, i)
            target_x = w * xh + (1 - w) * (1 - xh)
            target_z = (z + d + NZ) % NZ
            sib_out[i] = term(at(target_x, target_z, 1 - core)).astype(BF)
            sib_copy(i).start()
            own[i] = term(at(target_x, target_z, core))

        for k in range(16):
            pl.when(i == k + 1)(functools.partial(finish, k))
        return carry

    lax.fori_loop(0, 17, step, 0)

    x_copy.wait_recv()
    summed = (
        own[15] + sib_in[15].astype(F32) + z_in[15].astype(F32) + z_in2[1].astype(F32) + x_in[...].astype(F32)
    )
    own_rows = jnp.concatenate([gat[2 * col], gat[2 * col + 1]], axis=0).astype(F32)
    combined = (scal[...] * (summed + own_rows)).astype(BF)
    mixed = jnp.dot(combined, weight_ref[...], preferred_element_type=F32) + bias_ref[...]
    out_ref[...] = jnp.maximum(mixed, 0.0).astype(BF)

    for copy in sends:
        copy.wait_send()
    for i in range(16):
        sib_copy(i).wait_send()
        if DIST[i] == 4:
            z_copy(i, 0).wait_send()
            z_copy(i, 1).wait_send()
        elif DIST[i] != 0:
            z_copy(i).wait_send()
    x_copy.wait_send()


def local(features, degrees, blocks, block_ids, counts, weight, out_bias):
    vmem = pl.BlockSpec(memory_space=pltpu.VMEM)
    smem = pl.BlockSpec(memory_space=pltpu.SMEM)
    full = (ROWS, FEAT)
    dma = pltpu.SemaphoreType.DMA
    return pl.pallas_call(
        kernel,
        out_shape=jax.ShapeDtypeStruct(full, BF),
        in_specs=[vmem, vmem, pl.BlockSpec(memory_space=pl.ANY), smem, smem, vmem, vmem],
        out_specs=vmem,
        scratch_shapes=[
            pltpu.VMEM((16, BS, FEAT), BF),
            pltpu.VMEM((SEGS, SLOTS, BS, BS), BF),
            pltpu.VMEM((SEGS, ROWS, SLOTS * BS), BF),
            pltpu.VMEM((16,) + full, F32),
            pltpu.VMEM((16,) + full, BF),
            pltpu.VMEM((16,) + full, BF),
            pltpu.VMEM((16,) + full, BF),
            pltpu.VMEM((16,) + full, BF),
            pltpu.VMEM((2,) + full, BF),
            pltpu.VMEM(full, BF),
            pltpu.VMEM(full, BF),
            pltpu.VMEM((ROWS, 1), F32),
            dma((8,)), dma((14,)), dma((14,)), dma((16,)), dma((16,)), dma((16,)), dma((16,)), dma((2,)), dma((2,)),
            dma, dma,
        ],
        compiler_params=pltpu.CompilerParams(
            collective_id=0, has_side_effects=True, vmem_limit_bytes=60 * 1024 * 1024
        ),
        cost_estimate=pl.CostEstimate(
            flops=2 * SEGS * ROWS * SLOTS * BS * FEAT, bytes_accessed=SEGS * SLOTS * BS * BS * 2, transcendentals=0
        ),
    )(degrees.reshape(1, ROWS), features, blocks, block_ids, counts, weight, out_bias.reshape(1, FEAT))


def solution(mesh):
    placed = (
        P(("row", "col"), None),
        P(("row", "col")),
        P("row", "col", None, None),
        P("row", "col"),
        P("row", "col"),
        P(),
        P(),
    )
    return jax.shard_map(
        local, mesh=mesh, in_specs=placed, out_specs=P(("row", "col"), None), check_vma=False
    )
```

time: 386 us -> 56.4 us (0.15); the launches traced: 381 us -> 55.4 us
  waiting for transfers between devices: 169 us -> 0 us
  matrix products: 112 us -> 0 us
  local copies, waits for them, and re-layouts: 83.2 us -> 4.28 us
  Pallas kernels: 0 us -> 51.1 us
  between operations: 13.4 us -> 0.01 us
    reduce_scatter x1 -> x0, waiting for transfers between devices: 127 us -> none  [local(): lax.psum_scatter(partial_value.reshape(sub_count * seg_rows, partial_valu...]
    dot_general x17 -> x0, matrix products: 112 us -> none  [the longest x8 71.3 us: slot_term(): jnp.einsum('kr,kif->rif', select, products, precision=lax.Precision.HIGHEST)]
    gather x32 -> x0, local copies, waits for them, and re-layouts: 74.3 us -> none  [the longest x8 49 us: segment_term(): block_vals = lax.dynamic_index_in_dim(blocks, subrange, 0, keepdims=False)]
    pallas_call x0 -> x1, Pallas kernels: none -> 51.1 us  [local(): pl.pallas_call(kernel, out_shape=jax.ShapeDtypeStruct(full, BF), in_specs...]
    all_gather x1 -> x0, waiting for transfers between devices: 41.7 us -> none  [local(): gathered = lax.all_gather(scaled, 'col', axis=0, tiled=True)]
    dynamic_update_slice x8 -> x0, local copies, waits for them, and re-layouts: 6.82 us -> none  [local(): lax.map(segment_term, jnp.arange(sub_count, dtype=jnp.int32), batch_size=4)]
    unnamed x6 -> x3, local copies, waits for them, and re-layouts: 0.01 us -> 4.28 us
  transfers between devices with their start and end apart: 2 -> 0, of which waited for: 2 -> 0; matrix products, arithmetic and copies ran while one was open for 0% -> 0% of each run, Pallas kernels for 0% -> 0%
where the time goes in v1:
time: 56.4 us; the launch traced here: 55.4 us
  Pallas kernels  51.1 us (91%)
  local copies, waits for them, and re-layouts  4.28 us (8%)
    pallas_call x1, Pallas kernels, local(): pl.pallas_call(kernel, out_shape=jax.ShapeDtypeStruct(full, BF), in_specs...  51.1 us
    unnamed x3, local copies, waits for them, and re-layouts  4.28 us

profile of v1, /device:TPU:1, one launch (start us, length us, event | category | flops | bytes accessed | tf_op | source)
XLA Modules:
  0.0 55.4 jit_solution(4780483019463382640)
XLA Ops:
  0.0 1.4 %copy.8.ids_ref = s32[32,11]{1,0:T(8,128)} copy(s32[32,11]{0,1:T(8,128)} %param.10) | data formatting | bytes 2816 | tf_op args[3]
  1.4 1.3 %copy.9.cnt_ref = s32[32,1]{1,0:T(8,128)} copy(s32[32,1]{0,1:T(1,128)} %param.11) | data formatting | bytes 256 | tf_op args[4]
  2.7 51.1 %shard_map.73 = bf16[256,256]{1,0:T(8,128)(2,1)} custom-call(s32[1,256]{1,0:T(1,128)} %bitcast.2, bf16[256,256]{1,0:T(8,128)(2,1)} %feat_ref.1, bf16[32,11,128,128]{3,2,1,0:T(8,128)(2,1)} %blocks_ref.1, s32[32,11]{1,0:T(8,128)} %copy.8.ids_ref, s32[32,1]{1,0:T(8,128)} %copy.9.cnt_ref, bf16[256,256]{1,0:T(8,128)(2,1)} %weight_ref.1, f32[1,256]{1,0:T(1,128)} %bitcast.3), custom_call_target="tpu_custom_call" | custom-call | flops 5905580032 | bytes 11534336 | tf_op jit(solution)/shard_map/pallas_call | solution.py:253
  53.8 1.6 %copy.11 = bf16[256,256]{1,0:T(8,128)(2,1)} copy(bf16[256,256]{1,0:T(8,128)(2,1)} %shard_map.73) | data formatting | bytes 262144

commit v2 on v1

v2 whole, which is shorter than its diff:
```python
import functools

import jax
import jax.numpy as jnp
from jax import lax
from jax.experimental import pallas as pl
from jax.experimental.pallas import tpu as pltpu
from jax.sharding import PartitionSpec as P

MESH = pl.DeviceIdType.MESH
BF = jnp.bfloat16
F32 = jnp.float32
NZ = 8
NY = 4
SEGS = 32
SLOTS = 11
BS = 128
ROWS = 256
FEAT = 256
PIECES = 4
PIECE = ROWS // PIECES
X_FIRST = (0, 1)
HALF = [0, 1, 0, 0, 1, 1, 0, 0, 1, 1, 0, 0, 1, 1, 0, 1]
DIST = [4, 4, 3, -3, -3, 3, 2, -2, -2, 2, -1, 1, 1, -1, 0, 0]
TASK = {pair: i for i, pair in enumerate(zip(HALF, DIST))}
XSLOT = {d: i for i, d in enumerate((4, 3, -3, 2, -2, 1, -1, 0))}
FOLLOW = {
    3: [(0, 4, 1), (0, 4, 0), (0, 4, 3), (0, 4, 2)],
    4: [(1, 4, 3), (0, 3, 1), (0, 3, 0), (1, 4, 2), (0, 3, 3)],
    5: [(0, -3, 1), (0, -3, 0), (0, -3, 2)],
    6: [(1, 4, 1), (0, -3, 3), (0, 3, 2), (1, -3, 2), (1, 4, 0)],
    7: [(1, 3, 3), (1, 3, 2), (1, 3, 1), (1, -3, 3)],
    9: [(0, 2, 1), (0, 2, 0), (1, -3, 1), (1, -3, 0), (0, 2, 3), (0, -2, 1), (0, -2, 0), (0, 2, 2), (0, -2, 3),
        (1, 3, 0), (0, -2, 2)],
    10: [(1, -2, 2)],
    11: [(1, -2, 3)],
    12: [(1, 2, 3), (1, 2, 2), (1, 2, 1)],
    13: [(0, -1, 1), (0, -1, 0), (0, 1, 1), (0, 1, 0), (1, -2, 1), (0, 1, 3), (0, 1, 2), (1, -2, 0), (1, 2, 0),
         (0, -1, 3), (0, -1, 2)],
    15: [(1, 1, 3)],
    16: [(1, 1, 2), (1, -1, 3), (1, -1, 2), (1, -1, 1), (0, 0, 1), (0, 0, 0), (1, -1, 0), (1, 1, 1), (0, 0, 3),
         (1, 1, 0), (0, 0, 2), (1, 0, 1), (1, 0, 3), (1, 0, 0), (1, 0, 2)],
}


def pick(table, index):
    value = jnp.int32(table[0])
    for i in range(1, len(table)):
        value = jnp.where(index >= i, jnp.int32(table[i]), value)
    return value


def kernel(
    deg_hbm, feat_hbm, blocks_ref, ids_hbm, cnt_hbm, weight_hbm, bias_hbm, out_ref,
    deg_ref, feat_ref, ids_ref, cnt_ref, weight_ref, bias_ref,
    gat, stage, left, own, sib_out, sib_in, z_out, z_in, z_in2, x_in, scal,
    in_sem, stage_sem, ag_send, ag_recv, sib_send, sib_recv, z_send, z_recv, z_recv2, x_send, x_recv,
):
    row, col = lax.axis_index("row"), lax.axis_index("col")
    core = row % 2
    z = (row // 2) % NZ
    xh = row // (2 * NZ)
    y, xl = col // 2, col % 2

    def at(xh_, z_, core_):
        return xh_ * (2 * NZ) + z_ * 2 + core_

    z_up = (at(xh, (z + 1) % NZ, core), col)
    z_dn = (at(xh, (z + NZ - 1) % NZ, core), col)
    sib = (at(xh, z, 1 - core), col)
    x_far = (at(1 - xh, z, core), col)
    c_up = ((y + 1) % NY) * 2 + xl
    c_dn = ((y + NY - 1) % NY) * 2 + xl
    c_x = y * 2 + 1 - xl
    c_two = ((y + 2) % NY) * 2 + xl
    y_up, y_dn, x_near = (row, c_up), (row, c_dn), (row, c_x)

    barrier = pltpu.get_barrier_semaphore()
    for other in (z_up, z_dn, sib, x_far, y_up, y_dn, x_near):
        pl.semaphore_signal(barrier, inc=1, device_id=other, device_id_type=MESH)

    inputs = [
        pltpu.make_async_copy(src, dst, in_sem.at[i])
        for i, (src, dst) in enumerate((
            (deg_hbm, deg_ref), (feat_hbm, feat_ref), (ids_hbm, ids_ref), (cnt_hbm, cnt_ref),
            (weight_hbm, weight_ref), (bias_hbm, bias_ref),
        ))
    ]
    for copy in inputs:
        copy.start()
    loads = [
        pltpu.make_async_copy(
            blocks_ref.at[pl.ds(4 * i, 4)], stage.at[pl.ds(4 * i, 4)], stage_sem.at[i]
        )
        for i in range(8)
    ]
    for load in loads:
        load.start()
    inputs[0].wait()
    inputs[1].wait()

    rows = lax.broadcasted_iota(jnp.int32, (ROWS, ROWS), 0)
    cols = lax.broadcasted_iota(jnp.int32, (ROWS, ROWS), 1)
    degs = jnp.broadcast_to(deg_ref[...].astype(F32), (ROWS, ROWS))
    scaling = lax.rsqrt(jnp.sum(jnp.where(rows == cols, degs, 0.0), axis=1, keepdims=True))
    scal[...] = scaling
    scaled = (feat_ref[...].astype(F32) * scaling).astype(BF)
    gat[2 * col] = scaled[:BS]
    gat[2 * col + 1] = scaled[BS:]

    pl.semaphore_wait(barrier, 7)

    def piece_of(source, p):
        return gat.at[2 * source + p // 2, pl.ds((p % 2) * PIECE, PIECE)]

    def ag(source, p, send, recv, target):
        return pltpu.make_async_remote_copy(
            src_ref=piece_of(source, p), dst_ref=piece_of(source, p),
            send_sem=ag_send.at[send, p], recv_sem=ag_recv.at[recv, p],
            device_id=target, device_id_type=MESH,
        )

    FROM_DN, FROM_UP, FROM_X, TWO, X_DN, X_UP, X_TWO = range(7)
    source_of = {
        FROM_DN: c_dn, FROM_UP: c_up, FROM_X: c_x, TWO: c_two,
        X_DN: ((y + NY - 1) % NY) * 2 + 1 - xl, X_UP: ((y + 1) % NY) * 2 + 1 - xl, X_TWO: ((y + 2) % NY) * 2 + 1 - xl,
    }
    sends = []

    def send(*copies):
        for copy in copies:
            copy.start()
            sends.append(copy)

    def landed(kind, p):
        ag(source_of[kind], p, 0, kind, y_up).wait_recv()

    for a, b, c in zip((0, 2, 1, 3), (1, 3, 0, 2), (0, 1, 2, 3)):
        send(ag(col, a, 0, FROM_DN, y_up), ag(col, c, 2, FROM_X, x_near), ag(col, b, 1, FROM_UP, y_dn))

    def prepare(first, last):
        for i in range(first // 4, last // 4):
            loads[i].wait()

        def body(s, carry):
            live = cnt_ref[0, s]
            for k in range(SLOTS):
                q = ids_ref[k, s]
                block = stage[s, k]
                top = jnp.where((q < 16) & (k < live), 1.0, 0.0).astype(F32)
                low = jnp.where((q >= 16) & (k < live), 1.0, 0.0).astype(F32)
                left[s, :BS, k * BS:(k + 1) * BS] = block * jnp.full((BS, BS), top, F32).astype(BF)
                left[s, BS:, k * BS:(k + 1) * BS] = block * jnp.full((BS, BS), low, F32).astype(BF)
            return carry

        lax.fori_loop(first, last, body, 0)

    def relay_x(p):
        landed(FROM_X, p)
        send(ag(c_x, p, 3, X_DN, y_up), ag(c_x, p, 4, X_UP, y_dn))

    def relay_y(p):
        if p % 2 == 0:
            landed(FROM_DN, p)
            send(ag(c_dn, p, 5, TWO, y_up))
        else:
            landed(FROM_UP, p)
            send(ag(c_up, p, 5, TWO, y_dn))

    def relay_two(p):
        landed(TWO, p)
        send(ag(c_two, p, 6, X_TWO, x_near))

    inputs[2].wait()
    inputs[3].wait()
    prepare(0, 8)
    relay_y(0)
    relay_x(0)
    relay_y(1)
    relay_y(2)
    relay_x(1)
    relay_y(3)
    prepare(8, 12)
    relay_x(2)
    prepare(12, 16)
    relay_x(3)
    prepare(16, 20)
    relay_two(0)
    relay_two(1)
    prepare(20, 24)
    relay_two(2)
    relay_two(3)
    prepare(24, 32)
    for p in range(PIECES):
        landed(FROM_UP if p % 2 == 0 else FROM_DN, p)
        landed(X_DN, p)
        landed(X_UP, p)
    for p in range(PIECES):
        landed(X_TWO, p)
    inputs[4].wait()
    inputs[5].wait()

    def term(s):
        right = jnp.concatenate([gat[ids_ref[k, s] % 16] for k in range(SLOTS)], axis=0)
        return jnp.dot(left[s], right, preferred_element_type=F32)

    def sib_copy(i):
        return pltpu.make_async_remote_copy(
            src_ref=sib_out.at[i], dst_ref=sib_in.at[i], send_sem=sib_send.at[i], recv_sem=sib_recv.at[i],
            device_id=sib, device_id_type=MESH,
        )

    def part(p):
        return pl.ds(p * PIECE, PIECE)

    def x_copy(d, p):
        return pltpu.make_async_remote_copy(
            src_ref=z_out.at[TASK[0, d], part(p)], dst_ref=x_in.at[XSLOT[d], part(p)],
            send_sem=x_send.at[XSLOT[d], p], recv_sem=x_recv.at[XSLOT[d], p],
            device_id=x_far, device_id_type=MESH,
        )

    def z_copy(w, d, p):
        up = d > 0 and (d < 4 or p % 2 == 0)
        then = TASK[w, d - 1 if up else -3 if d == 4 else d + 1]
        down_last = d == -1
        return pltpu.make_async_remote_copy(
            src_ref=z_out.at[TASK[w, d], part(p)],
            dst_ref=z_in2.at[w, part(p)] if down_last else z_in.at[then, part(p)],
            send_sem=z_send.at[TASK[w, d], p],
            recv_sem=z_recv2.at[w, p] if down_last else z_recv.at[then, p],
            device_id=z_up if up else z_dn, device_id_type=MESH,
        )

    def next_hop(w, d, p):
        if w == 0 and (p in X_FIRST or d == 0):
            return x_copy(d, p)
        return None if d == 0 else z_copy(w, d, p)

    waited = set()

    def finish(w, d, p):
        i = TASK[w, d]
        if i not in waited:
            waited.add(i)
            sib_copy(i).wait_recv()
        value = own[i, part(p)] + sib_in[i, part(p)].astype(F32)
        if w == 1 and (p in X_FIRST or d == 0):
            x_copy(d, p).wait_recv()
            value = value + x_in[XSLOT[d], part(p)].astype(F32)
        if w == 1 or p not in X_FIRST:
            from_dn = d in (0, 1, 2) or (d == 3 and p % 2 == 0)
            from_up = d in (-1, -2) or (d == -3 and p % 2 == 1)
            if from_dn:
                z_copy(w, d + 1, p).wait_recv()
            if from_up:
                z_copy(w, 4 if d == -3 else d - 1, p).wait_recv()
            if from_dn or from_up:
                value = value + z_in[i, part(p)].astype(F32)
            if d == 0:
                z_copy(w, -1, p).wait_recv()
                value = value + z_in2[w, part(p)].astype(F32)
        copy = next_hop(w, d, p)
        if copy is not None:
            z_out[i, part(p)] = value.astype(BF)
            copy.start()
            return
        mine = gat[2 * col + p // 2, pl.ds((p % 2) * PIECE, PIECE)].astype(F32)
        combined = (scal[part(p)] * (value + mine)).astype(BF)
        mixed = jnp.dot(combined, weight_ref[...], preferred_element_type=F32) + bias_ref[...]
        out_ref[part(p)] = jnp.maximum(mixed, 0.0).astype(BF)

    def follow(made):
        for piece in FOLLOW[made]:
            finish(*piece)

    def step(i, carry):
        w, d = pick(HALF, i), pick(DIST, i)
        target_x = w * xh + (1 - w) * (1 - xh)
        target_z = (z + d + NZ) % NZ
        sib_out[i] = term(at(target_x, target_z, 1 - core)).astype(BF)
        sib_copy(i).start()
        own[i] = term(at(target_x, target_z, core))

        for made in FOLLOW:
            if made < 16:
                pl.when(i == made - 1)(functools.partial(follow, made))
        return carry

    lax.fori_loop(0, 16, step, 0)
    follow(16)

    for copy in sends:
        copy.wait_send()
    for i, (w, d) in enumerate(zip(HALF, DIST)):
        sib_copy(i).wait_send()
        for p in range(PIECES):
            copy = next_hop(w, d, p)
            if copy is not None:
                copy.wait_send()


def local(features, degrees, blocks, block_ids, counts, weight, out_bias):
    vmem = pl.BlockSpec(memory_space=pltpu.VMEM)
    anywhere = pl.BlockSpec(memory_space=pl.ANY)
    full = (ROWS, FEAT)
    dma = pltpu.SemaphoreType.DMA
    return pl.pallas_call(
        kernel,
        out_shape=jax.ShapeDtypeStruct(full, BF),
        in_specs=[anywhere] * 7,
        out_specs=vmem,
        scratch_shapes=[
            pltpu.VMEM((1, ROWS), jnp.int32),
            pltpu.VMEM(full, BF),
            pltpu.SMEM((SLOTS, SEGS), jnp.int32),
            pltpu.SMEM((1, SEGS), jnp.int32),
            pltpu.VMEM((FEAT, FEAT), BF),
            pltpu.VMEM((1, FEAT), F32),
            pltpu.VMEM((16, BS, FEAT), BF),
            pltpu.VMEM((SEGS, SLOTS, BS, BS), BF),
            pltpu.VMEM((SEGS, ROWS, SLOTS * BS), BF),
            pltpu.VMEM((16,) + full, F32),
            pltpu.VMEM((16,) + full, BF),
            pltpu.VMEM((16,) + full, BF),
            pltpu.VMEM((16,) + full, BF),
            pltpu.VMEM((16,) + full, BF),
            pltpu.VMEM((2,) + full, BF),
            pltpu.VMEM((8,) + full, BF),
            pltpu.VMEM((ROWS, 1), F32),
            dma((6,)), dma((8,)), dma((7, PIECES)), dma((7, PIECES)), dma((16,)), dma((16,)),
            dma((16, PIECES)), dma((16, PIECES)), dma((2, PIECES)), dma((8, PIECES)), dma((8, PIECES)),
        ],
        compiler_params=pltpu.CompilerParams(
            collective_id=0, has_side_effects=True, vmem_limit_bytes=60 * 1024 * 1024
        ),
        cost_estimate=pl.CostEstimate(
            flops=2 * SEGS * ROWS * SLOTS * BS * FEAT, bytes_accessed=SEGS * SLOTS * BS * BS * 2, transcendentals=0
        ),
    )(degrees.reshape(1, ROWS), features, blocks, block_ids.T, counts.T, weight, out_bias.reshape(1, FEAT))


def solution(mesh):
    placed = (
        P(("row", "col"), None),
        P(("row", "col")),
        P("row", "col", None, None),
        P("row", "col"),
        P("row", "col"),
        P(),
        P(),
    )
    return jax.shard_map(
        local, mesh=mesh, in_specs=placed, out_specs=P(("row", "col"), None), check_vma=False
    )
```

time: 56.4 us -> 51.6 us (0.915); the launches traced: 55.4 us -> 51.5 us
  local copies, waits for them, and re-layouts: 4.28 us -> 1.57 us
  Pallas kernels: 51.1 us -> 49.9 us
    unnamed x3 -> x1, local copies, waits for them, and re-layouts: 4.28 us -> 1.57 us
    pallas_call x1, Pallas kernels: 51.1 us -> 49.9 us  [local(): pl.pallas_call(kernel, out_shape=jax.ShapeDtypeStruct(full, BF), in_specs...]
where the time goes in v2:
time: 51.6 us; the launch traced here: 51.5 us
  Pallas kernels  49.9 us (97%)
  local copies, waits for them, and re-layouts  1.57 us (3%)
    pallas_call x1, Pallas kernels, local(): pl.pallas_call(kernel, out_shape=jax.ShapeDtypeStruct(full, BF), in_specs...  49.9 us
    unnamed x1, local copies, waits for them, and re-layouts  1.57 us

profile of v2, /device:TPU:1, one launch (start us, length us, event | category | flops | bytes accessed | tf_op | source)
XLA Modules:
  0.0 51.5 jit_solution(16926334607063980564)
XLA Ops:
  0.0 49.9 %shard_map.73 = bf16[256,256]{1,0:T(8,128)(2,1)} custom-call(s32[1,256]{1,0:T(1,128)} %bitcast.5, bf16[256,256]{1,0:T(8,128)(2,1)} %feat_hbm.1, bf16[32,11,128,128]{3,2,1,0:T(8,128)(2,1)} %blocks_ref.1, s32[11,32]{1,0:T(8,128)} %bitcast.4, s32[1,32]{1,0:T(1,128)} %bitcast.7, bf16[256,256]{1,0:T(8,128)(2,1)} %weight_hbm.1, f32[1,256]{1,0:T(1,128)} %bitcast.6), custom_call_target="tpu_custom_call" | custom-call | flops 5905580032 | bytes 11534336 | tf_op jit(solution)/shard_map/pallas_call | solution.py:308
  49.9 1.6 %copy.9 = bf16[256,256]{1,0:T(8,128)(2,1)} copy(bf16[256,256]{1,0:T(8,128)(2,1)} %shard_map.73) | data formatting | bytes 262144

commit v3 on v2

--- a/solution.py
+++ b/solution.py
@@ -278,9 +278,11 @@
         w, d = pick(HALF, i), pick(DIST, i)
         target_x = w * xh + (1 - w) * (1 - xh)
         target_z = (z + d + NZ) % NZ
-        sib_out[i] = term(at(target_x, target_z, 1 - core)).astype(BF)
+        theirs = term(at(target_x, target_z, 1 - core))
+        ours = term(at(target_x, target_z, core))
+        sib_out[i] = theirs.astype(BF)
+        own[i] = ours
         sib_copy(i).start()
-        own[i] = term(at(target_x, target_z, core))
 
         for made in FOLLOW:
             if made < 16:

time: 51.6 us -> 48.9 us (0.948)
  Pallas kernels: 49.9 us -> 47.3 us
    pallas_call x1, Pallas kernels: 49.9 us -> 47.3 us  [local(): pl.pallas_call(kernel, out_shape=jax.ShapeDtypeStruct(full, BF), in_specs...]
where the time goes in v3:
time: 48.9 us
  Pallas kernels  47.3 us (97%)
  local copies, waits for them, and re-layouts  1.57 us (3%)
    pallas_call x1, Pallas kernels, local(): pl.pallas_call(kernel, out_shape=jax.ShapeDtypeStruct(full, BF), in_specs...  47.3 us
    unnamed x1, local copies, waits for them, and re-layouts  1.57 us

profile of v3, /device:TPU:1, one launch (start us, length us, event | category | flops | bytes accessed | tf_op | source)
XLA Modules:
  0.0 48.9 jit_solution(1889886042833923224)
XLA Ops:
  0.0 47.3 %shard_map.73 = bf16[256,256]{1,0:T(8,128)(2,1)} custom-call(s32[1,256]{1,0:T(1,128)} %bitcast.5, bf16[256,256]{1,0:T(8,128)(2,1)} %feat_hbm.1, bf16[32,11,128,128]{3,2,1,0:T(8,128)(2,1)} %blocks_ref.1, s32[11,32]{1,0:T(8,128)} %bitcast.4, s32[1,32]{1,0:T(1,128)} %bitcast.7, bf16[256,256]{1,0:T(8,128)(2,1)} %weight_hbm.1, f32[1,256]{1,0:T(1,128)} %bitcast.6), custom_call_target="tpu_custom_call" | custom-call | flops 5905580032 | bytes 11534336 | tf_op jit(solution)/shard_map/pallas_call | solution.py:310
  47.3 1.6 %copy.9 = bf16[256,256]{1,0:T(8,128)(2,1)} copy(bf16[256,256]{1,0:T(8,128)(2,1)} %shard_map.73) | data formatting | bytes 262144

commit v4 on v3

--- a/solution.py
+++ b/solution.py
@@ -19,6 +19,7 @@
 FEAT = 256
 PIECES = 4
 PIECE = ROWS // PIECES
+BY_X = (0,)
 X_FIRST = (0, 1)
 HALF = [0, 1, 0, 0, 1, 1, 0, 0, 1, 1, 0, 0, 1, 1, 0, 1]
 DIST = [4, 4, 3, -3, -3, 3, 2, -2, -2, 2, -1, 1, 1, -1, 0, 0]
@@ -73,10 +74,10 @@
     c_dn = ((y + NY - 1) % NY) * 2 + xl
     c_x = y * 2 + 1 - xl
     c_two = ((y + 2) % NY) * 2 + xl
-    y_up, y_dn, x_near = (row, c_up), (row, c_dn), (row, c_x)
+    y_up, y_dn, y_two, x_near = (row, c_up), (row, c_dn), (row, c_two), (row, c_x)
 
     barrier = pltpu.get_barrier_semaphore()
-    for other in (z_up, z_dn, sib, x_far, y_up, y_dn, x_near):
+    for other in (z_up, z_dn, sib, x_far, y_up, y_dn, y_two, x_near):
         pl.semaphore_signal(barrier, inc=1, device_id=other, device_id_type=MESH)
 
     inputs = [
@@ -108,7 +109,7 @@
     gat[2 * col] = scaled[:BS]
     gat[2 * col + 1] = scaled[BS:]
 
-    pl.semaphore_wait(barrier, 7)
+    pl.semaphore_wait(barrier, 8)
 
     def piece_of(source, p):
         return gat.at[2 * source + p // 2, pl.ds((p % 2) * PIECE, PIECE)]
@@ -135,8 +136,10 @@
     def landed(kind, p):
         ag(source_of[kind], p, 0, kind, y_up).wait_recv()
 
-    for a, b, c in zip((0, 2, 1, 3), (1, 3, 0, 2), (0, 1, 2, 3)):
-        send(ag(col, a, 0, FROM_DN, y_up), ag(col, c, 2, FROM_X, x_near), ag(col, b, 1, FROM_UP, y_dn))
+    for p in range(PIECES):
+        send(ag(col, p, 5, TWO, y_two), ag(col, p, 2, FROM_X, x_near))
+    for p in range(PIECES):
+        send(ag(col, p, 0, FROM_DN, y_up), ag(col, p, 1, FROM_UP, y_dn))
 
     def prepare(first, last):
         for i in range(first // 4, last // 4):
@@ -157,46 +160,40 @@
 
     def relay_x(p):
         landed(FROM_X, p)
-        send(ag(c_x, p, 3, X_DN, y_up), ag(c_x, p, 4, X_UP, y_dn))
-
-    def relay_y(p):
-        if p % 2 == 0:
-            landed(FROM_DN, p)
-            send(ag(c_dn, p, 5, TWO, y_up))
-        else:
-            landed(FROM_UP, p)
-            send(ag(c_up, p, 5, TWO, y_dn))
+        if p not in BY_X:
+            send(ag(c_x, p, 3, X_DN, y_up), ag(c_x, p, 4, X_UP, y_dn))
 
     def relay_two(p):
         landed(TWO, p)
         send(ag(c_two, p, 6, X_TWO, x_near))
 
+    def relay_y(p):
+        landed(FROM_DN, p)
+        landed(FROM_UP, p)
+        if p in BY_X:
+            send(ag(c_dn, p, 3, X_DN, x_near), ag(c_up, p, 4, X_UP, x_near))
+
     inputs[2].wait()
     inputs[3].wait()
     prepare(0, 8)
-    relay_y(0)
     relay_x(0)
-    relay_y(1)
-    relay_y(2)
+    relay_two(0)
+    prepare(8, 12)
     relay_x(1)
-    relay_y(3)
-    prepare(8, 12)
+    relay_two(1)
+    prepare(12, 16)
     relay_x(2)
-    prepare(12, 16)
+    relay_two(2)
     relay_x(3)
-    prepare(16, 20)
-    relay_two(0)
-    relay_two(1)
-    prepare(20, 24)
-    relay_two(2)
     relay_two(3)
+    prepare(16, 24)
+    for p in range(PIECES):
+        relay_y(p)
     prepare(24, 32)
     for p in range(PIECES):
-        landed(FROM_UP if p % 2 == 0 else FROM_DN, p)
+        landed(X_TWO, p)
         landed(X_DN, p)
         landed(X_UP, p)
-    for p in range(PIECES):
-        landed(X_TWO, p)
     inputs[4].wait()
     inputs[5].wait()
 
@@ -309,7 +306,7 @@
     dma = pltpu.SemaphoreType.DMA
     return pl.pallas_call(
         kernel,
-        out_shape=jax.ShapeDtypeStruct(full, BF),
+        out_shape=pltpu.VMEM(full, BF),
         in_specs=[anywhere] * 7,
         out_specs=vmem,
         scratch_shapes=[

time: 48.9 us -> 46.1 us (0.943)
  Pallas kernels: 47.3 us -> 45.4 us
  local copies, waits for them, and re-layouts: 1.57 us -> 0.66 us
    pallas_call x1, Pallas kernels: 47.3 us -> 45.4 us  [local(): pl.pallas_call(kernel, out_shape=pltpu.VMEM(full, BF), in_specs=[anywhere...]
    unnamed x1, local copies, waits for them, and re-layouts: 1.57 us -> 0.66 us
where the time goes in v4:
time: 46.1 us
  Pallas kernels  45.4 us (98%)
  local copies, waits for them, and re-layouts  0.66 us (1%)
    pallas_call x1, Pallas kernels, local(): pl.pallas_call(kernel, out_shape=pltpu.VMEM(full, BF), in_specs=[anywhere...  45.4 us

profile of v4, /device:TPU:1, one launch (start us, length us, event | category | flops | bytes accessed | tf_op | source)
XLA Modules:
  0.0 46.1 jit_solution(13688106039486879889)
XLA Ops:
  0.0 45.4 %shard_map.73 = bf16[256,256]{1,0:T(8,128)(2,1)S(1)} custom-call(s32[1,256]{1,0:T(1,128)} %bitcast.5, bf16[256,256]{1,0:T(8,128)(2,1)} %feat_hbm.1, bf16[32,11,128,128]{3,2,1,0:T(8,128)(2,1)} %blocks_ref.1, s32[11,32]{1,0:T(8,128)} %bitcast.4, s32[1,32]{1,0:T(1,128)} %bitcast.7, bf16[256,256]{1,0:T(8,128)(2,1)} %weight_hbm.1, f32[1,256]{1,0:T(1,128)} %bitcast.6), custom_call_target="tpu_custom_call" | custom-call | flops 5905580032 | bytes 11534336 | tf_op jit(solution)/shard_map/pallas_call | solution.py:307
  45.4 0.7 %copy.9 = bf16[256,256]{1,0:T(8,128)(2,1)} copy(bf16[256,256]{1,0:T(8,128)(2,1)S(1)} %shard_map.73) | data formatting | bytes 262144

commit v5 on v4

--- a/solution.py
+++ b/solution.py
@@ -21,26 +21,26 @@
 PIECE = ROWS // PIECES
 BY_X = (0,)
 X_FIRST = (0, 1)
-HALF = [0, 1, 0, 0, 1, 1, 0, 0, 1, 1, 0, 0, 1, 1, 0, 1]
-DIST = [4, 4, 3, -3, -3, 3, 2, -2, -2, 2, -1, 1, 1, -1, 0, 0]
+HALF = [0, 1, 0, 0, 0, 1, 1, 0, 1, 1, 0, 0, 0, 1, 1, 1]
+DIST = [4, 4, -3, 3, -2, 3, -3, 2, 2, -2, -1, 1, 0, -1, 1, 0]
 TASK = {pair: i for i, pair in enumerate(zip(HALF, DIST))}
 XSLOT = {d: i for i, d in enumerate((4, 3, -3, 2, -2, 1, -1, 0))}
 FOLLOW = {
-    3: [(0, 4, 1), (0, 4, 0), (0, 4, 3), (0, 4, 2)],
-    4: [(1, 4, 3), (0, 3, 1), (0, 3, 0), (1, 4, 2), (0, 3, 3)],
+    3: [(0, 4, 3), (0, 4, 2), (0, 4, 0), (0, 4, 1)],
+    4: [(1, 4, 3), (1, 4, 2)],
     5: [(0, -3, 1), (0, -3, 0), (0, -3, 2)],
-    6: [(1, 4, 1), (0, -3, 3), (0, 3, 2), (1, -3, 2), (1, 4, 0)],
-    7: [(1, 3, 3), (1, 3, 2), (1, 3, 1), (1, -3, 3)],
-    9: [(0, 2, 1), (0, 2, 0), (1, -3, 1), (1, -3, 0), (0, 2, 3), (0, -2, 1), (0, -2, 0), (0, 2, 2), (0, -2, 3),
-        (1, 3, 0), (0, -2, 2)],
-    10: [(1, -2, 2)],
-    11: [(1, -2, 3)],
-    12: [(1, 2, 3), (1, 2, 2), (1, 2, 1)],
-    13: [(0, -1, 1), (0, -1, 0), (0, 1, 1), (0, 1, 0), (1, -2, 1), (0, 1, 3), (0, 1, 2), (1, -2, 0), (1, 2, 0),
-         (0, -1, 3), (0, -1, 2)],
-    15: [(1, 1, 3)],
-    16: [(1, 1, 2), (1, -1, 3), (1, -1, 2), (1, -1, 1), (0, 0, 1), (0, 0, 0), (1, -1, 0), (1, 1, 1), (0, 0, 3),
-         (1, 1, 0), (0, 0, 2), (1, 0, 1), (1, 0, 3), (1, 0, 0), (1, 0, 2)],
+    6: [(0, 3, 0), (0, 3, 3), (0, 3, 1)],
+    7: [(0, -3, 3), (1, 4, 0), (0, -2, 1), (0, -2, 0), (0, 3, 2), (1, 3, 3), (1, 4, 1)],
+    8: [(1, 3, 2), (1, -3, 2), (1, -3, 3)],
+    9: [(0, -2, 2), (1, -3, 0)],
+    10: [(0, 2, 3), (0, 2, 0), (0, 2, 1), (0, -2, 3), (1, 3, 0), (1, 3, 1)],
+    11: [(1, -3, 1), (0, 2, 2)],
+    12: [(1, -2, 2), (1, 2, 3)],
+    13: [(0, -1, 0), (1, -2, 3), (0, -1, 1), (1, 2, 2), (0, -1, 2), (0, 1, 3), (0, 1, 1), (0, 1, 0)],
+    14: [(1, -2, 0), (1, 2, 0), (0, -1, 3), (0, 0, 1), (0, 0, 0), (1, 2, 1)],
+    15: [(1, -2, 1), (0, 1, 2)],
+    16: [(1, -1, 2), (1, -1, 3), (1, 1, 3), (1, 1, 2), (1, -1, 0), (1, 1, 0), (0, 0, 3), (1, 1, 1), (1, -1, 1),
+        (0, 0, 2), (1, 0, 0), (1, 0, 3), (1, 0, 1), (1, 0, 2)],
 }
 
 

time: 46.1 us -> 44.6 us (0.967)
  Pallas kernels: 45.4 us -> 43.8 us
    pallas_call x1, Pallas kernels: 45.4 us -> 43.8 us  [local(): pl.pallas_call(kernel, out_shape=pltpu.VMEM(full, BF), in_specs=[anywhere...]
where the time goes in v5:
time: 44.6 us; the launch traced here: 44.5 us
  Pallas kernels  43.8 us (98%)
  local copies, waits for them, and re-layouts  0.66 us (1%)
    pallas_call x1, Pallas kernels, local(): pl.pallas_call(kernel, out_shape=pltpu.VMEM(full, BF), in_specs=[anywhere...  43.8 us

profile of v5, /device:TPU:1, one launch (start us, length us, event | category | flops | bytes accessed | tf_op | source)
XLA Modules:
  0.0 44.5 jit_solution(4409921579261727561)
XLA Ops:
  0.0 43.8 %shard_map.73 = bf16[256,256]{1,0:T(8,128)(2,1)S(1)} custom-call(s32[1,256]{1,0:T(1,128)} %bitcast.5, bf16[256,256]{1,0:T(8,128)(2,1)} %feat_hbm.1, bf16[32,11,128,128]{3,2,1,0:T(8,128)(2,1)} %blocks_ref.1, s32[11,32]{1,0:T(8,128)} %bitcast.4, s32[1,32]{1,0:T(1,128)} %bitcast.7, bf16[256,256]{1,0:T(8,128)(2,1)} %weight_hbm.1, f32[1,256]{1,0:T(1,128)} %bitcast.6), custom_call_target="tpu_custom_call" | custom-call | flops 5905580032 | bytes 11534336 | tf_op jit(solution)/shard_map/pallas_call | solution.py:307
  43.8 0.7 %copy.9 = bf16[256,256]{1,0:T(8,128)(2,1)} copy(bf16[256,256]{1,0:T(8,128)(2,1)S(1)} %shard_map.73) | data formatting | bytes 262144

commit v6 on v5

--- a/solution.py
+++ b/solution.py
@@ -186,10 +186,10 @@
     relay_two(2)
     relay_x(3)
     relay_two(3)
-    prepare(16, 24)
-    for p in range(PIECES):
+    relay_y(0)
+    prepare(16, 32)
+    for p in range(1, PIECES):
         relay_y(p)
-    prepare(24, 32)
     for p in range(PIECES):
         landed(X_TWO, p)
         landed(X_DN, p)

time: 44.6 us -> 44.2 us (level)
  no operation moved by 1% of the time
where the time goes in v6:
time: 44.2 us; the launch traced here: 44.1 us
  Pallas kernels  43.4 us (98%)
  local copies, waits for them, and re-layouts  0.66 us (1%)
    pallas_call x1, Pallas kernels, local(): pl.pallas_call(kernel, out_shape=pltpu.VMEM(full, BF), in_specs=[anywhere...  43.4 us

profile of v6, /device:TPU:1, one launch (start us, length us, event | category | flops | bytes accessed | tf_op | source)
XLA Modules:
  0.0 44.1 jit_solution(1173695548049096906)
XLA Ops:
  0.0 43.4 %shard_map.73 = bf16[256,256]{1,0:T(8,128)(2,1)S(1)} custom-call(s32[1,256]{1,0:T(1,128)} %bitcast.5, bf16[256,256]{1,0:T(8,128)(2,1)} %feat_hbm.1, bf16[32,11,128,128]{3,2,1,0:T(8,128)(2,1)} %blocks_ref.1, s32[11,32]{1,0:T(8,128)} %bitcast.4, s32[1,32]{1,0:T(1,128)} %bitcast.7, bf16[256,256]{1,0:T(8,128)(2,1)} %weight_hbm.1, f32[1,256]{1,0:T(1,128)} %bitcast.6), custom_call_target="tpu_custom_call" | custom-call | flops 5905580032 | bytes 11534336 | tf_op jit(solution)/shard_map/pallas_call | solution.py:307
  43.4 0.7 %copy.9 = bf16[256,256]{1,0:T(8,128)(2,1)} copy(bf16[256,256]{1,0:T(8,128)(2,1)S(1)} %shard_map.73) | data formatting | bytes 262144

commit v7 on v6

--- a/solution.py
+++ b/solution.py
@@ -21,26 +21,26 @@
 PIECE = ROWS // PIECES
 BY_X = (0,)
 X_FIRST = (0, 1)
-HALF = [0, 1, 0, 0, 0, 1, 1, 0, 1, 1, 0, 0, 0, 1, 1, 1]
-DIST = [4, 4, -3, 3, -2, 3, -3, 2, 2, -2, -1, 1, 0, -1, 1, 0]
+HALF = [0, 1, 0, 0, 1, 1, 0, 0, 1, 1, 0, 0, 1, 0, 1, 1]
+DIST = [4, 4, 3, -3, -3, 3, -2, 2, -2, 2, -1, 1, 1, 0, -1, 0]
 TASK = {pair: i for i, pair in enumerate(zip(HALF, DIST))}
 XSLOT = {d: i for i, d in enumerate((4, 3, -3, 2, -2, 1, -1, 0))}
 FOLLOW = {
-    3: [(0, 4, 3), (0, 4, 2), (0, 4, 0), (0, 4, 1)],
-    4: [(1, 4, 3), (1, 4, 2)],
-    5: [(0, -3, 1), (0, -3, 0), (0, -3, 2)],
-    6: [(0, 3, 0), (0, 3, 3), (0, 3, 1)],
-    7: [(0, -3, 3), (1, 4, 0), (0, -2, 1), (0, -2, 0), (0, 3, 2), (1, 3, 3), (1, 4, 1)],
-    8: [(1, 3, 2), (1, -3, 2), (1, -3, 3)],
-    9: [(0, -2, 2), (1, -3, 0)],
-    10: [(0, 2, 3), (0, 2, 0), (0, 2, 1), (0, -2, 3), (1, 3, 0), (1, 3, 1)],
+    3: [(0, 4, 0), (0, 4, 2), (0, 4, 3), (0, 4, 1)],
+    4: [(1, 4, 2), (1, 4, 3)],
+    5: [(0, 3, 0), (0, 3, 1), (0, 3, 3)],
+    6: [(0, -3, 2), (0, -3, 0), (0, -3, 1)],
+    7: [(1, 4, 0), (0, -3, 3), (0, 3, 2), (1, 4, 1), (1, -3, 2), (1, 3, 3), (1, 3, 2), (1, -3, 3)],
+    8: [(0, -2, 0), (0, -2, 1)],
+    9: [(1, 3, 1), (0, -2, 2)],
+    10: [(0, 2, 3), (0, 2, 1), (1, 3, 0), (0, -2, 3), (0, 2, 0), (1, -3, 0)],
     11: [(1, -3, 1), (0, 2, 2)],
-    12: [(1, -2, 2), (1, 2, 3)],
-    13: [(0, -1, 0), (1, -2, 3), (0, -1, 1), (1, 2, 2), (0, -1, 2), (0, 1, 3), (0, 1, 1), (0, 1, 0)],
-    14: [(1, -2, 0), (1, 2, 0), (0, -1, 3), (0, 0, 1), (0, 0, 0), (1, 2, 1)],
+    12: [(1, 2, 3), (1, -2, 2)],
+    13: [(1, 2, 2), (1, -2, 3), (0, -1, 0), (0, -1, 2), (0, -1, 1), (1, 2, 1), (0, 1, 0), (0, 1, 1)],
+    14: [(0, 1, 3), (0, -1, 3), (1, 2, 0), (1, -2, 0)],
     15: [(1, -2, 1), (0, 1, 2)],
-    16: [(1, -1, 2), (1, -1, 3), (1, 1, 3), (1, 1, 2), (1, -1, 0), (1, 1, 0), (0, 0, 3), (1, 1, 1), (1, -1, 1),
-        (0, 0, 2), (1, 0, 0), (1, 0, 3), (1, 0, 1), (1, 0, 2)],
+    16: [(1, 1, 3), (0, 0, 1), (0, 0, 0), (1, 1, 2), (1, -1, 3), (1, -1, 2), (0, 0, 3), (1, 1, 1), (1, 1, 0),
+        (1, -1, 0), (0, 0, 2), (1, -1, 1), (1, 0, 3), (1, 0, 0), (1, 0, 2), (1, 0, 1)],
 }
 
 

time: 44.2 us -> 44 us (level)
  no operation moved by 1% of the time
where the time goes in v7:
time: 44 us; the launch traced here: 43.9 us
  Pallas kernels  43.2 us (98%)
  local copies, waits for them, and re-layouts  0.66 us (2%)
    pallas_call x1, Pallas kernels, local(): pl.pallas_call(kernel, out_shape=pltpu.VMEM(full, BF), in_specs=[anywhere...  43.2 us

profile of v7, /device:TPU:1, one launch (start us, length us, event | category | flops | bytes accessed | tf_op | source)
XLA Modules:
  0.0 43.9 jit_solution(13632150786105616077)
XLA Ops:
  0.0 43.2 %shard_map.73 = bf16[256,256]{1,0:T(8,128)(2,1)S(1)} custom-call(s32[1,256]{1,0:T(1,128)} %bitcast.5, bf16[256,256]{1,0:T(8,128)(2,1)} %feat_hbm.1, bf16[32,11,128,128]{3,2,1,0:T(8,128)(2,1)} %blocks_ref.1, s32[11,32]{1,0:T(8,128)} %bitcast.4, s32[1,32]{1,0:T(1,128)} %bitcast.7, bf16[256,256]{1,0:T(8,128)(2,1)} %weight_hbm.1, f32[1,256]{1,0:T(1,128)} %bitcast.6), custom_call_target="tpu_custom_call" | custom-call | flops 5905580032 | bytes 11534336 | tf_op jit(solution)/shard_map/pallas_call | solution.py:307
  43.2 0.7 %copy.9 = bf16[256,256]{1,0:T(8,128)(2,1)} copy(bf16[256,256]{1,0:T(8,128)(2,1)S(1)} %shard_map.73) | data formatting | bytes 262144
